TPU v7x, 768 devices: a whole 4x8x12 slice. The times are simulated.
768 devices in a mesh: dp: 384 (over z, y, x), fsdp: 2 (over core).
Axes of the slice: x: 4, y: 8, z: 12, core: 2. Of those that a mesh axis runs over, the one named last changes fastest.
Arguments:
- patches: bfloat16 [196608, 1280], P(('dp', 'fsdp')), may hold values from -6 to 6
- queries: bfloat16 [196608, 1280], P(('dp', 'fsdp')), may hold values from -200 to 200
- key_in: bfloat16 [196608, 1280], P(('dp', 'fsdp')), may hold values from -200 to 200
- values: bfloat16 [196608, 1280], P(('dp', 'fsdp')), may hold values from -6 to 6
- windows: int32 [768, 256], P(('dp', 'fsdp')), may hold values from 0 to 7, never falling along the last dimension, each value on 1 to 64 neighbouring positions
- out_weight: bfloat16 [1280, 1280], P('fsdp'), may hold values from -0.15625 to 0.15625
- owners: int32 [196608, 1], P(('dp', 'fsdp')), may hold values from 0 to 1; in each aligned block of 256 rows (0 to 255, 256 to 511, ...) at most 256 rows name the same one
- grad_out: bfloat16 [196608, 1280], P(('dp', 'fsdp')), may hold values from -6 to 6
Outputs:
- returned: bfloat16 [393216, 1280], P(('dp', 'fsdp'))
- grad_wo: float32 [1280, 1280], P('fsdp')
Inputs may be any that keep to these rules, and one draw needn't show every extreme that they name: `windows`: window ids never fall along a device's rows; each window holds 1 to 64 rows, some window exactly 64. `owners`: among the rows of one device at most 256 name the same owner, and in every draw some device's owner takes exactly 256.
All inputs are finite; a program needn't handle non-finite values.
Results may differ from a plain program's by a relative error of at most 0.007.
Values may be sent and summed in bfloat16 or wider, within the bound.
A program may use at most 64 MiB of HBM per device.

v0:
```python
import math

import jax
import jax.numpy as jnp
from jax import lax
from jax.sharding import PartitionSpec as P

HEADS = 16
HEAD_DIM = 80


def attend(queries, key_in, values, window_ids):
    length = queries.shape[0]
    query_heads = queries.reshape(length, HEADS, HEAD_DIM)
    key_heads = key_in.reshape(length, HEADS, HEAD_DIM)
    value_heads = values.reshape(length, HEADS, HEAD_DIM)
    scores = jnp.einsum(
        "qhd,khd->hqk", query_heads, key_heads, preferred_element_type=jnp.float32
    ) / math.sqrt(HEAD_DIM)
    same_window = window_ids[:, None] == window_ids[None, :]
    scores = jnp.where(same_window[None], scores, -1e30)
    highest = jnp.max(scores, axis=-1, keepdims=True)
    expo = jnp.exp(scores - highest)
    weights = (expo / jnp.sum(expo, axis=-1, keepdims=True)).astype(jnp.bfloat16)
    attended = jnp.einsum("hqk,khd->qhd", weights, value_heads, preferred_element_type=jnp.float32)
    return attended.reshape(length, HEADS * HEAD_DIM).astype(jnp.bfloat16)


def place_rows(encoded, owner_ids, groups, capacity):
    onehot = (owner_ids[:, None] == jnp.arange(groups, dtype=jnp.int32)[None, :]).astype(jnp.int32)
    ranking = jnp.sum((jnp.cumsum(onehot, axis=0) - 1) * onehot, axis=1)
    positions = owner_ids * capacity + ranking
    empty = jnp.zeros((groups * capacity, encoded.shape[1]), jnp.bfloat16)
    return empty.at[positions].set(encoded)


def per_device(patches, queries, key_in, values, windows, out_weight, owners, grad_out):
    length = patches.shape[0]
    groups = lax.axis_size("fsdp")
    replicas = lax.axis_size("dp")
    capacity = 2 * length // groups
    attended = attend(queries, key_in, values, windows[0])
    columns = attended
    projected = jnp.dot(
        columns,
        lax.all_gather(out_weight, "fsdp", axis=0, tiled=True),
        preferred_element_type=jnp.float32,
    )
    encoded = (patches.astype(jnp.float32) + projected).astype(jnp.bfloat16)
    buffer = place_rows(encoded, owners[:, 0], groups, capacity)
    returned = lax.all_to_all(buffer, "fsdp", split_axis=0, concat_axis=0, tiled=True)
    columns = attended
    partial_value = lax.dot_general(
        columns, grad_out, (((0,), (0,)), ((), ())), preferred_element_type=jnp.float32
    )
    shard_sum = lax.psum_scatter(
        lax.optimization_barrier(partial_value.astype(jnp.bfloat16))
        .astype(jnp.float32)
        .astype(jnp.bfloat16),
        "fsdp",
        scatter_dimension=0,
        tiled=True,
    ).astype(jnp.float32)
    summed = lax.psum(shard_sum, "dp")
    factor = 1.0 / math.sqrt(length * groups * replicas)
    grad_wo = summed * factor
    return (returned, grad_wo)


def solution(mesh):
    return jax.shard_map(
        per_device,
        mesh=mesh,
        in_specs=(
            P(("dp", "fsdp"), None),
            P(("dp", "fsdp"), None),
            P(("dp", "fsdp"), None),
            P(("dp", "fsdp"), None),
            P(("dp", "fsdp"), None),
            P("fsdp", None),
            P(("dp", "fsdp"), None),
            P(("dp", "fsdp"), None),
        ),
        out_specs=(P(("dp", "fsdp"), None), P("fsdp", None)),
        check_vma=False,
    )
```

profile of v0, /device:TPU:4, one launch (start us, length us, event | category | flops | bytes accessed | tf_op | source)
XLA Modules:
  0.0 2159.7 jit_solution(9309217378102319074)
XLA Ops:
  7.2 0.0 all-gather.2.cloned.1.call-start
  7.3 0.7 all-gather.2.cloned.1.call-update
  7.9 0.0 reduce-scatter.2.cloned.1.call-start
  8.0 1.3 copy.14
  9.3 1.1 copy.15
  10.4 0.2 copy.16
  10.7 0.1 broadcast_compare_fusion
  10.8 4.5 fusion.15
  15.3 2.7 fusion.7
  18.0 2.7 convolution_convert_fusion
  20.8 0.0 reduce-scatter.2.cloned.1.call-update
  20.8 0.7 copy-done.3
  21.4 0.6 reduce-window.6
  22.1 0.2 slice_reduce_fusion
  22.3 0.2 reduce-window.9
  22.4 0.1 add_bitcast_fusion
  22.6 17.8 all-gather.2.cloned.1.call-done
  40.3 3.8 fusion.2
  44.1 2.7 scatter_custom_fusion
  46.8 4.8 all_to_all.12
  51.6 15.6 reduce-scatter.2.cloned.1.call-done
  67.3 2080.6 %all-reduce.1 = f32[640,1280]{1,0:T(8,128)} all-reduce(bf16[640,1280]{1,0:T(8,128)(2,1)} %reduce-scatter.2.cloned.1.call-done), channel_id=1, replica_groups=mesh['dp'=384,'fsdp'=2] {'dp'}, use_global_device_ids=true, to_apply=%region_7.8 | all-reduce | flops 819200 | bytes 4915200 | tf_op jit(solution)/shard_map/psum | solution.py:64
  2147.9 3.9 broadcast_multiply_fusion
  2151.8 1.1 copy.24
  (14 shorter events, 0.1 us)
Async XLA Ops:
  7.2 10.9 copy-start
  7.2 2.1 copy-start.1
  7.2 3.2 copy-start.2
  7.2 3.5 copy-start.4
  7.2 33.1 %all-gather.2.cloned.1.call-start = ((), (), s32[]{:S(2)}) async-start(), calls=%async_computation.2 | async-start | bytes 4915200 | tf_op jit(solution)/shard_map/all_gather | solution.py:46
  7.9 59.3 %reduce-scatter.2.cloned.1.call-start = ((), (), s32[]{:S(2)}) async-start(), calls=%async_computation.3 | async-start | bytes 4915200 | tf_op jit(solution)/shard_map/reduce_scatter | solution.py:56
  20.8 0.7 copy-start.3
  20.8 19.6 copy-start.5
Sparse Core Ops, SparseCore 0:
  10.4 29.8 all-gather.1
  44.0 23.2 reduce-scatter.1
where the time goes:
time: 2160 us
  blocking collectives  2090 us (97%)
  waiting for transfers between devices  34.1 us (2%)
    psum x1, blocking collectives, per_device(): summed = lax.psum(shard_sum, 'dp')  2080 us
  transfers between devices with their start and end apart: 2, of which 2 were waited for; matrix products, arithmetic and copies ran while one was open for 1% of the time, Pallas kernels for 0%

commit v1 on v0

--- a/solution.py
+++ b/solution.py
@@ -3,6 +3,7 @@
 import jax
 import jax.numpy as jnp
 from jax import lax
+from jax.sharding import Mesh
 from jax.sharding import PartitionSpec as P
 
 HEADS = 16
@@ -37,7 +38,7 @@
 def per_device(patches, queries, key_in, values, windows, out_weight, owners, grad_out):
     length = patches.shape[0]
     groups = lax.axis_size("fsdp")
-    replicas = lax.axis_size("dp")
+    replicas = lax.axis_size("x") * lax.axis_size("y") * lax.axis_size("z")
     capacity = 2 * length // groups
     attended = attend(queries, key_in, values, windows[0])
     columns = attended
@@ -61,26 +62,23 @@
         scatter_dimension=0,
         tiled=True,
     ).astype(jnp.float32)
-    summed = lax.psum(shard_sum, "dp")
+    piece = lax.psum_scatter(shard_sum, "x", scatter_dimension=0, tiled=True)
+    piece = lax.psum_scatter(piece, "y", scatter_dimension=1, tiled=True)
+    piece = lax.psum(piece, "z")
+    piece = lax.all_gather(piece, "y", axis=1, tiled=True)
+    summed = lax.all_gather(piece, "x", axis=0, tiled=True)
     factor = 1.0 / math.sqrt(length * groups * replicas)
     grad_wo = summed * factor
     return (returned, grad_wo)
 
 
 def solution(mesh):
+    grid = Mesh(mesh.devices.reshape(12, 8, 4, 2), ("z", "y", "x", "fsdp"))
+    rows = P(("z", "y", "x", "fsdp"), None)
     return jax.shard_map(
         per_device,
-        mesh=mesh,
-        in_specs=(
-            P(("dp", "fsdp"), None),
-            P(("dp", "fsdp"), None),
-            P(("dp", "fsdp"), None),
-            P(("dp", "fsdp"), None),
-            P(("dp", "fsdp"), None),
-            P("fsdp", None),
-            P(("dp", "fsdp"), None),
-            P(("dp", "fsdp"), None),
-        ),
-        out_specs=(P(("dp", "fsdp"), None), P("fsdp", None)),
+        mesh=grid,
+        in_specs=(rows, rows, rows, rows, rows, P("fsdp", None), rows, rows),
+        out_specs=(rows, P("fsdp", None)),
         check_vma=False,
     )

time: 2160 us -> 352 us (0.16)
  the two profiles are of different devices: /device:TPU:4 before, /device:TPU:1 now
where the time goes in v1:
time: 352 us
  waiting for transfers between devices  267 us (76%)
  blocking collectives  35.8 us (10%)
  between operations  14.2 us (4%)
  local copies, waits for them, and re-layouts  14 us (4%)
  matrix products  11.8 us (3%)
  other arithmetic  9.06 us (3%)
    psum x1, waiting for transfers between devices, per_device(): piece = lax.psum(piece, 'z')  108 us
    reduce_scatter x1, waiting for transfers between devices, per_device(): piece = lax.psum_scatter(shard_sum, 'x', scatter_dimension=0, tiled=True)  47.6 us
    unnamed x7, waiting for transfers between devices  41.8 us
    all_gather x1, waiting for transfers between devices, per_device(): summed = lax.all_gather(piece, 'x', axis=0, tiled=True)  32.9 us
    reduce_scatter x1, waiting for transfers between devices, per_device(): lax.psum_scatter(lax.optimization_barrier(partial_value.astype(jnp.bfloat...  31.3 us
    all_gather x1, blocking collectives, per_device(): piece = lax.all_gather(piece, 'y', axis=1, tiled=True)  23 us
    all_to_all x1, blocking collectives, per_device(): lax.all_to_all(buffer, 'fsdp', split_axis=0, concat_axis=0, tiled=True)  12.7 us
    unnamed x12, local copies, waits for them, and re-layouts  9.4 us
  transfers between devices with their start and end apart: 6, of which 6 were waited for; matrix products, arithmetic and copies ran while one was open for 2% of the time, Pallas kernels for 0%

profile of v1, /device:TPU:1, one launch (start us, length us, event | category | flops | bytes accessed | tf_op | source)
XLA Modules:
  0.0 352.0 jit_solution(14869354264719980413)
XLA Ops:
  7.2 1.4 copy.24
  8.6 1.3 copy.25
  9.9 0.9 broadcast_compare_fusion
  10.8 1.3 copy.26
  12.1 3.4 fusion.15
  15.6 2.7 fusion.7
  18.3 2.7 convolution_convert_fusion
  21.1 31.3 %reduce-scatter.6.cloned.1.call-done = bf16[640,1280]{1,0:T(8,128)(2,1)} async-done(((bf16[1280,1280]{1,0:T(8,128)(2,1)}), bf16[640,1280]{1,0:T(8,128)(2,1)}) %reduce-scatter.6.cloned.1.call-update) | async-done | bytes 1638416 | tf_op jit(solution)/shard_map/reduce_scatter | solution.py:57
  52.4 3.4 convert_element_type.39
  55.9 47.6 %reduce-scatter.8.cloned.1.call-done = f32[160,1280]{1,0:T(8,128)} async-done(((f32[640,1280]{1,0:T(8,128)}), f32[160,1280]{1,0:T(8,128)}) %reduce-scatter.8.cloned.1.call-update) | async-done | bytes 819216 | tf_op jit(solution)/shard_map/reduce_scatter | solution.py:65
  103.5 2.6 copy.31
  106.2 41.2 %reduce-scatter.10.cloned.1.call-done = f32[160,160]{1,0:T(8,128)} async-done(((f32[1280,160]{1,0:T(8,128)}), f32[160,160]{1,0:T(8,128)}) %reduce-scatter.10.cloned.1.call-update) | async-done | bytes 102416
  147.4 1.7 copy.32
  149.7 108.1 %all-reduce.2.cloned.1.call-done = f32[160,160]{1,0:T(8,128)} async-done(((f32[160,160]{1,0:T(8,128)}), f32[160,160]{1,0:T(8,128)}) %all-reduce.2.cloned.1.call-update) | async-done | bytes 102416 | tf_op jit(solution)/shard_map/psum | solution.py:67
  257.8 1.0 copy.28
  258.9 23.0 %all_gather.10 = f32[160,1280]{0,1:T(8,128)S(1)} all-gather(f32[160,160]{0,1:T(8,128)S(1)} %copy.28), channel_id=1, replica_groups=mesh['z'=12,'y'=8,'x'=4,'fsdp'=2] {'y'}, dimensions={1}, use_global_device_ids=true | all-gather | bytes 921600 | tf_op jit(solution)/shard_map/all_gather | solution.py:68
  281.9 1.3 copy.29
  284.3 5.1 %all-gather.3.cloned.1.call-done = bf16[1280,1280]{1,0:T(8,128)(2,1)} async-done(((bf16[640,1280]{1,0:T(8,128)(2,1)}), bf16[1280,1280]{1,0:T(8,128)(2,1)}) %all-gather.3.cloned.1.call-update) | async-done | bytes 3276816 | tf_op jit(solution)/shard_map/all_gather | solution.py:47
  289.5 3.0 fusion.2
  292.4 2.1 scatter_custom_fusion
  294.6 12.7 %all_to_all.12 = bf16[2,256,1280]{2,1,0:T(8,128)(2,1)S(1)} all-to-all(bf16[2,256,1280]{2,1,0:T(8,128)(2,1)S(1)} %bitcast.37), channel_id=1, replica_groups=mesh['z'=12,'y'=8,'x'=4,'fsdp'=2] {'fsdp'}, dimensions={0} | all-to-all | bytes 2621440 | tf_op jit(solution)/shard_map/all_to_all | solution.py:52
  307.3 32.9 %all-gather.5.cloned.1.call-done = f32[640,1280]{1,0:T(8,128)} async-done(((f32[160,1280]{1,0:T(8,128)}), f32[640,1280]{1,0:T(8,128)}) %all-gather.5.cloned.1.call-update) | async-done | bytes 3276816 | tf_op jit(solution)/shard_map/all_gather | solution.py:69
  340.2 3.9 %broadcast_multiply_fusion = f32[640,1280]{1,0:T(8,128)} fusion(f32[640,1280]{1,0:T(8,128)} %all-gather.5.cloned.1.call-done), kind=kLoop, calls=%fused_computation.13 | loop fusion | flops 819200 | bytes 6553600 | tf_op jit(solution)/shard_map/mul | solution.py:71
  344.1 1.1 copy.37
  (25 shorter events, 2.0 us)
Async XLA Ops:
  7.2 11.1 %copy-start = (bf16[256,1280]{1,0:T(8,128)(2,1)S(1)}, bf16[256,1280]{1,0:T(8,128)(2,1)}, u32[]{:S(2)}) copy-start(bf16[256,1280]{1,0:T(8,128)(2,1)} %param.15) | copy-start | bytes 1966084
  7.2 45.2 %reduce-scatter.6.cloned.1.call-start = ((), (), s32[]{:S(2)}) async-start(), calls=%async_computation.5 | async-start | bytes 4915200 | tf_op jit(solution)/shard_map/reduce_scatter | solution.py:57
  21.0 82.5 %reduce-scatter.8.cloned.1.call-start = ((), (), s32[]{:S(2)}) async-start(), calls=%async_computation.6 | async-start | bytes 4096000 | tf_op jit(solution)/shard_map/reduce_scatter | solution.py:65
  55.8 91.6 %reduce-scatter.10.cloned.1.call-start = ((), (), s32[]{:S(2)}) async-start(), calls=%async_computation.9 | async-start | bytes 1474560
  106.1 151.7 %all-reduce.2.cloned.1.call-start = ((), (), s32[]{:S(2)}) async-start(), calls=%async_computation.7 | async-start | bytes 327680 | tf_op jit(solution)/shard_map/psum | solution.py:67
  149.1 134.1 %copy-start.1 = (s32[256,1]{0,1:T(1,128)S(1)}, s32[256,1]{0,1:T(1,128)}, u32[]{:S(2)}) copy-start(s32[256,1]{0,1:T(1,128)} %param.14) | copy-start | bytes 3076
  149.1 140.4 %copy-start.2 = (bf16[256,1280]{1,0:T(8,128)(2,1)S(1)}, bf16[256,1280]{1,0:T(8,128)(2,1)}, u32[]{:S(2)}) copy-start(bf16[256,1280]{1,0:T(8,128)(2,1)} %param.8) | copy-start | bytes 1966084
  149.1 140.4 %all-gather.3.cloned.1.call-start = ((), (), s32[]{:S(2)}) async-start(), calls=%async_computation.4 | async-start | bytes 4915200 | tf_op jit(solution)/shard_map/all_gather | solution.py:47
  149.7 190.5 %all-gather.5.cloned.1.call-start = ((), (), s32[]{:S(2)}) async-start(), calls=%async_computation.8 | async-start | bytes 4096000 | tf_op jit(solution)/shard_map/all_gather | solution.py:69
Sparse Core Ops, SparseCore 0:
  21.1 31.2 reduce-scatter.5
  56.4 47.0 reduce-scatter.7
  107.5 39.8 reduce-scatter.9
  150.3 107.5 all-reduce.1
  260.1 29.3 all-gather.2
  292.3 47.8 all-gather.4

commit v2 on v1

v2 whole, which is shorter than its diff:
```python
import functools
import math

import jax
import jax.numpy as jnp
from jax import lax
from jax.experimental import pallas as pl
from jax.experimental.pallas import tpu as pltpu
from jax.sharding import Mesh
from jax.sharding import PartitionSpec as P

HEADS = 16
HEAD_DIM = 80
MESH = pl.DeviceIdType.MESH
ROW, LANE = 16, 128
PARTS = ((7, ("x", "y", "z")), (3, ("y", "x", "z")))


def attend(queries, key_in, values, window_ids):
    length = queries.shape[0]
    query_heads = queries.reshape(length, HEADS, HEAD_DIM)
    key_heads = key_in.reshape(length, HEADS, HEAD_DIM)
    value_heads = values.reshape(length, HEADS, HEAD_DIM)
    scores = jnp.einsum(
        "qhd,khd->hqk", query_heads, key_heads, preferred_element_type=jnp.float32
    ) / math.sqrt(HEAD_DIM)
    same_window = window_ids[:, None] == window_ids[None, :]
    scores = jnp.where(same_window[None], scores, -1e30)
    highest = jnp.max(scores, axis=-1, keepdims=True)
    expo = jnp.exp(scores - highest)
    weights = (expo / jnp.sum(expo, axis=-1, keepdims=True)).astype(jnp.bfloat16)
    attended = jnp.einsum("hqk,khd->qhd", weights, value_heads, preferred_element_type=jnp.float32)
    return attended.reshape(length, HEADS * HEAD_DIM).astype(jnp.bfloat16)


class Part:
    def __init__(self, first, blocks, order, sizes, rows):
        self.first, self.blocks, self.order = first, blocks, order
        self.per_block = rows // ROW
        self.tiles = blocks * self.per_block
        n = [sizes[axis] for axis in order]
        self.n = n
        t1 = -(-self.tiles // n[0])
        t2 = -(-t1 // n[1])
        t3 = -(-t2 // n[2])
        t2 = -(-t2 // t3) * t3
        t1 = -(-t1 // t2) * t2
        self.take = (t1, t2, t3)
        self.owners = (-(-self.tiles // t1), t1 // t2, t2 // t3)
        self.padded = self.owners[0] * t1

    def scratch(self):
        held = {"sum0": pltpu.VMEM((self.padded, ROW, LANE), jnp.bfloat16)}
        for k in range(3):
            n, take = self.n[k], self.take[k]
            held[f"in{k}"] = pltpu.VMEM((n - 1, take, ROW, LANE), jnp.bfloat16)
            if k < 2:
                held[f"sum{k + 1}"] = pltpu.VMEM((take, ROW, LANE), jnp.bfloat16)
            for name in ("rs_send", "rs_recv", "ag_send", "ag_recv"):
                held[f"{name}{k}"] = pltpu.SemaphoreType.DMA((n - 1,))
        held["all"] = pltpu.VMEM((self.padded, ROW, LANE), jnp.bfloat16)
        return held


def among(condition, always, step):
    if always:
        step()
    else:
        pl.when(condition)(step)


def reduce_copies(part, held, k):
    axis, n, take, owners = part.order[k], part.n[k], part.take[k], part.owners[k]
    me = lax.axis_index(axis)
    for d in range(1, n):
        peer = lax.rem(me + d, n)
        run = peer if owners == n else jnp.minimum(peer, owners - 1)
        yield pltpu.make_async_remote_copy(
            src_ref=held[f"sum{k}"].at[pl.ds(run * take, take)],
            dst_ref=held[f"in{k}"].at[d - 1],
            send_sem=held[f"rs_send{k}"].at[d - 1],
            recv_sem=held[f"rs_recv{k}"].at[d - 1],
            device_id={axis: peer},
            device_id_type=MESH,
        ), peer < owners, me < owners


def reduce_start(part, held, k):
    always = part.owners[k] == part.n[k]
    for copy, sent, _ in reduce_copies(part, held, k):
        among(sent, always, copy.start)


def reduce_finish(part, held, k, base):
    n, take, owners = part.n[k], part.take[k], part.owners[k]
    me = lax.axis_index(part.order[k])

    def receive():
        for copy, _, _ in reduce_copies(part, held, k):
            copy.wait_recv()
        total = held[f"sum{k}"][pl.ds(me * take, take)].astype(jnp.float32)
        for d in range(1, n):
            total += held[f"in{k}"][d - 1].astype(jnp.float32)
        total = total.astype(jnp.bfloat16)
        if k < 2:
            held[f"sum{k + 1}"][...] = total
        else:
            held["all"][pl.ds(base, take)] = total

    among(me < owners, owners == n, receive)


def gather_copy(part, held, k, bases, d, run):
    axis, n, take, owners = part.order[k], part.n[k], part.take[k], part.owners[k]
    start = bases[k] + (run if owners == n else jnp.minimum(run, owners - 1)) * take
    return pltpu.make_async_remote_copy(
        src_ref=held["all"].at[pl.ds(start, take)],
        dst_ref=held["all"].at[pl.ds(start, take)],
        send_sem=held[f"ag_send{k}"].at[d - 1],
        recv_sem=held[f"ag_recv{k}"].at[d - 1],
        device_id={axis: lax.rem(lax.axis_index(axis) + d, n)},
        device_id_type=MESH,
    )


def gather_sent(part, held, k, bases):
    me, n = lax.axis_index(part.order[k]), part.n[k]
    for d in range(1, n):
        yield gather_copy(part, held, k, bases, d, me), me < part.owners[k]


def gather_received(part, held, k, bases):
    me, n = lax.axis_index(part.order[k]), part.n[k]
    for d in range(1, n):
        source = lax.rem(me + n - d, n)
        yield gather_copy(part, held, k, bases, d, source), source < part.owners[k]


def gather_start(part, held, k, bases):
    always = part.owners[k] == part.n[k]
    for copy, sent in gather_sent(part, held, k, bases):
        among(sent, always, copy.start)


def gather_finish(part, held, k, bases):
    always = part.owners[k] == part.n[k]
    for copy, received in gather_received(part, held, k, bases):
        among(received, always, copy.wait_recv)


def drain(part, held, bases):
    for k in range(3):
        always = part.owners[k] == part.n[k]
        for copy, sent, _ in reduce_copies(part, held, k):
            among(sent, always, copy.wait_send)
        for copy, sent in gather_sent(part, held, k, bases):
            among(sent, always, copy.wait_send)


def exchange(
    parts, sizes, factor,
    attended, grad_out, weight, patches, owner_ids,
    returned, gradient,
    near, scratch,
):
    core = lax.axis_index("fsdp")
    other = 1 - core
    half = weight.shape[0]
    length = attended.shape[0]
    mine = pl.ds(pl.multiple_of(core * half, LANE), half)
    theirs = pl.ds(pl.multiple_of(other * half, LANE), half)
    sems = near["sems"]

    barrier = pltpu.get_barrier_semaphore()
    greeted = 0
    for axis, n in sizes.items():
        me = lax.axis_index(axis)
        for d in range(1, n):
            pl.semaphore_signal(
                barrier, inc=1, device_id={axis: lax.rem(me + d, n)}, device_id_type=MESH
            )
            greeted += 1

    def local(source, target, number):
        copy = pltpu.make_async_copy(source, target, sems.at[number])
        copy.start()
        return copy

    weight_here = local(weight, near["weight"].at[0], 0)
    patches_here = local(patches, near["patches"], 1)

    pl.semaphore_wait(barrier, greeted)

    def across(source, target, number):
        copy = pltpu.make_async_remote_copy(
            src_ref=source,
            dst_ref=target,
            send_sem=sems.at[number],
            recv_sem=sems.at[number + 1],
            device_id={"fsdp": other},
            device_id_type=MESH,
        )
        copy.start()
        return copy

    attended_there = across(attended.at[:, theirs], near["attended"], 2)
    grad_out_there = across(grad_out, near["grad_out"], 4)
    weight_there = across(weight, near["weight"].at[1], 6)

    attended_there.wait_recv()
    grad_out_there.wait_recv()
    rows_in = (((0,), (0,)), ((), ()))
    for part, held in zip(parts, scratch):
        columns = pl.ds(part.first * LANE, part.blocks * LANE)
        product = lax.dot_general(
            attended[:, mine], grad_out[:, columns], rows_in, preferred_element_type=jnp.float32
        ) + lax.dot_general(
            near["attended"][...], near["grad_out"][:, columns], rows_in,
            preferred_element_type=jnp.float32,
        )
        product = product.astype(jnp.bfloat16)
        for block in range(part.blocks):
            held["sum0"][pl.ds(block * part.per_block, part.per_block)] = product[
                :, block * LANE:(block + 1) * LANE
            ].reshape(part.per_block, ROW, LANE)
        spare = part.padded - part.tiles
        if spare:
            held["sum0"][pl.ds(part.tiles, spare)] = jnp.zeros((spare, ROW, LANE), jnp.bfloat16)
        reduce_start(part, held, 0)

    weight_here.wait()
    patches_here.wait()
    weight_there.wait_recv()
    projected = jnp.dot(
        attended[:, mine], near["weight"][0], preferred_element_type=jnp.float32
    ) + jnp.dot(attended[:, theirs], near["weight"][1], preferred_element_type=jnp.float32)
    encoded = (near["patches"][...].astype(jnp.float32) + projected).astype(jnp.bfloat16)
    owner = owner_ids[...]
    earlier = (
        lax.broadcasted_iota(jnp.int32, (length, length), 0)
        < lax.broadcasted_iota(jnp.int32, (length, length), 1)
    ).astype(jnp.bfloat16)
    is_one = jnp.broadcast_to(owner, (ROW, length)).astype(jnp.float32).astype(jnp.bfloat16)
    ones_before = jnp.dot(is_one, earlier, preferred_element_type=jnp.float32)[:1]
    ones_before = ones_before.astype(jnp.int32)
    place = lax.broadcasted_iota(jnp.int32, (1, length), 1)
    rank = jnp.where(owner == 1, ones_before, place - ones_before)
    slot = lax.broadcasted_iota(jnp.int32, (length, length), 0)

    def placed(group):
        chosen = jnp.where(owner == group, rank, -1)
        onehot = (slot == chosen).astype(jnp.float32).astype(jnp.bfloat16)
        return jnp.dot(onehot, encoded, preferred_element_type=jnp.float32).astype(jnp.bfloat16)

    own_rows = pl.ds(pl.multiple_of(core * length, LANE), length)
    other_rows = pl.ds(pl.multiple_of(other * length, LANE), length)
    near["leaving"][...] = placed(other)
    rows_there = across(near["leaving"], near["returned"].at[own_rows], 8)
    near["returned"][own_rows] = placed(core)

    bases = []
    for part in parts:
        i1, i2, i3 = (lax.axis_index(axis) for axis in part.order)
        (t1, t2, t3), (_, m2, m3) = part.take, part.owners
        bases.append((0, i1 * t1, i1 * t1 + i2 * t2, i1 * t1 + i2 * t2 + i3 * t3))

    for k in range(3):
        for part, held, base in zip(parts, scratch, bases):
            reduce_finish(part, held, k, base[3])
            if k < 2:
                reduce_start(part, held, k + 1)
            else:
                gather_start(part, held, 2, base)
        if k == 0:
            rows_there.wait_recv()
            rows_out = local(near["returned"], returned, 10)
    for k in (2, 1, 0):
        for part, held, base in zip(parts, scratch, bases):
            gather_finish(part, held, k, base)
            if k > 0:
                gather_start(part, held, k - 1, base)
            else:
                for block in range(part.blocks):
                    tiles = held["all"][pl.ds(block * part.per_block, part.per_block)]
                    gradient[:, pl.ds((part.first + block) * LANE, LANE)] = (
                        tiles.reshape(half, LANE).astype(jnp.float32) * factor
                    )
    for part, held, base in zip(parts, scratch, bases):
        drain(part, held, base)
    for copy in (attended_there, grad_out_there, weight_there, rows_there):
        copy.wait_send()
    rows_out.wait()


def per_device(patches, queries, key_in, values, windows, out_weight, owners, grad_out):
    sizes = {axis: lax.axis_size(axis) for axis in ("fsdp", "x", "y", "z")}
    length, width = patches.shape
    half = out_weight.shape[0]
    attended = attend(queries, key_in, values, windows[0])
    parts, first = [], 0
    for blocks, order in PARTS:
        parts.append(Part(first, blocks, order, sizes, half))
        first += blocks
    factor = 1.0 / math.sqrt(length * math.prod(sizes.values()))
    bf16 = jnp.bfloat16
    near = {
        "weight": pltpu.VMEM((2, half, width), bf16),
        "patches": pltpu.VMEM((length, width), bf16),
        "attended": pltpu.VMEM((length, half), bf16),
        "grad_out": pltpu.VMEM((length, width), bf16),
        "leaving": pltpu.VMEM((length, width), bf16),
        "returned": pltpu.VMEM((2 * length, width), bf16),
        "sems": pltpu.SemaphoreType.DMA((11,)),
    }
    vmem, anywhere = (pl.BlockSpec(memory_space=space) for space in (pltpu.VMEM, pl.ANY))
    return pl.pallas_call(
        functools.partial(exchange, parts, sizes, factor),
        out_shape=(
            jax.ShapeDtypeStruct((2 * length, width), bf16),
            jax.ShapeDtypeStruct((half, width), jnp.float32),
        ),
        in_specs=[vmem, vmem, anywhere, anywhere, vmem],
        out_specs=(anywhere, vmem),
        scratch_shapes=[near, [part.scratch() for part in parts]],
        compiler_params=pltpu.CompilerParams(
            collective_id=0, has_side_effects=True, vmem_limit_bytes=48 * 1024 * 1024
        ),
    )(attended, grad_out, out_weight, patches, owners.reshape(1, length))


def solution(mesh):
    chips = mesh.devices.reshape(12, 8, 4, 2)
    grid = Mesh(chips, ("z", "y", "x", "fsdp"))
    rows = P(("z", "y", "x", "fsdp"), None)
    return jax.shard_map(
        per_device,
        mesh=grid,
        in_specs=(rows, rows, rows, rows, rows, P("fsdp", None), rows, rows),
        out_specs=(rows, P("fsdp", None)),
        check_vma=False,
    )
```

time: 352 us -> 103 us (0.29)
  the two profiles are of different devices: /device:TPU:1 before, /device:TPU:16 now
where the time goes in v2:
time: 103 us
  Pallas kernels  82.8 us (80%)
  local copies, waits for them, and re-layouts  11.3 us (11%)
  matrix products  7.12 us (7%)
    pallas_call x1, Pallas kernels, per_device(): pl.pallas_call(functools.partial(exchange, parts, sizes, factor), out_sha...  82.8 us
    unnamed x13, local copies, waits for them, and re-layouts  9.97 us
    dot_general x1, matrix products, attend(): jnp.einsum('hqk,khd->qhd', weights, value_heads, preferred_element_type=j...  3.67 us
    sub x1, matrix products, attend(): expo = jnp.exp(scores - highest)  3.45 us

profile of v2, /device:TPU:16, one launch (start us, length us, event | category | flops | bytes accessed | tf_op | source)
XLA Modules:
  0.0 102.8 jit_solution(16535510305761159207)
XLA Ops:
  0.6 0.9 broadcast_compare_fusion
  1.5 1.3 %copy.15 = bf16[256,1280]{0,1:T(8,128)(2,1)S(1)} copy(bf16[256,1280]{1,0:T(8,128)(2,1)} %param.9) | data formatting | bytes 1310720 | tf_op args[1]
  2.8 1.3 %copy.16 = bf16[256,1280]{0,1:T(8,128)(2,1)S(1)} copy(bf16[256,1280]{1,0:T(8,128)(2,1)} %param.10) | data formatting | bytes 1310720 | tf_op args[2]
  4.2 1.3 %copy.17 = bf16[256,1280]{0,1:T(8,128)(2,1)S(1)} copy(bf16[256,1280]{1,0:T(8,128)(2,1)} %param.11) | data formatting | bytes 1310720 | tf_op args[3]
  5.5 3.4 %fusion.11 = (f32[16,256]{1,0:T(8,128)S(1)}, f32[16,256,256]{1,2,0:T(8,128)}) fusion(pred[256,256]{0,1:T(8,128)(4,1)S(1)} %broadcast_compare_fusion, bf16[256,16,80]{0,2,1:T(8,128)(2,1)S(1)} %bitcast.15, bf16[256,16,80]{0,2,1:T(8,128)(2,1)S(1)} %bitcast.16), kind=kOutput, calls=%fused_computation.14 | convolution fusion | flops 171966720 | bytes 5586944 | tf_op jit(solution)/shard_map/sub | solution.py:30
  8.9 0.0 copy-start
  8.9 0.0 copy-start.1
  8.9 0.0 copy-start.3
  8.9 3.7 %fusion.6 = bf16[16,256,80]{1,2,0:T(8,128)(2,1)} fusion(bf16[256,16,80]{0,2,1:T(8,128)(2,1)S(1)} %bitcast.14, f32[16,256,256]{1,2,0:T(8,128)} %get-tuple-element.3, f32[16,256]{1,0:T(8,128)S(1)} %get-tuple-element.2), kind=kOutput, calls=%fused_computation.9 | convolution fusion | flops 170196992 | bytes 5521408 | tf_op jit(solution)/shard_map/hqk,khd->qhd/dot_general | solution.py:32
  12.6 1.3 %copy.19.attended = bf16[256,1280]{1,0:T(8,128)(2,1)S(1)} copy(bf16[256,1280]{0,1:T(8,128)(2,1)} %bitcast.17) | data formatting | bytes 1310720 | tf_op jit(solution)/shard_map/convert_element_type | solution.py:33
  13.9 0.0 copy-done
  14.0 0.0 copy-done.1
  14.0 0.0 copy-done.3
  14.0 0.0 copy-start.2
  14.0 1.1 %copy-done.2 = bf16[256,1280]{1,0:T(8,128)(2,1)S(1)} copy-done((bf16[256,1280]{1,0:T(8,128)(2,1)S(1)}, bf16[256,1280]{1,0:T(8,128)(2,1)}, u32[]{:S(2)}) %copy-start.2) | copy-done | bytes 655384
  15.1 82.8 %shard_map.95 = (bf16[512,1280]{1,0:T(8,128)(2,1)S(1)}, f32[640,1280]{1,0:T(8,128)}) custom-call(bf16[256,1280]{1,0:T(8,128)(2,1)S(1)} %copy.19.attended, bf16[256,1280]{1,0:T(8,128)(2,1)S(1)} %copy-done.1, bf16[640,1280]{1,0:T(8,128)(2,1)S(1)} %copy-done, bf16[256,1280]{1,0:T(8,128)(2,1)S(1)} %copy-done.2, s32[1,256]{1,0:T(1,128)S(1)} %bitcast.13), custom_call_target="tpu_custom_call" | custom-call | tf_op jit(solution)/shard_map/pallas_call | solution.py:316
  97.9 1.1 %copy.23 = bf16[512,1280]{1,0:T(8,128)(2,1)} copy(bf16[512,1280]{1,0:T(8,128)(2,1)S(1)} %get-tuple-element.6) | data formatting | bytes 2621440
  99.0 3.8 %copy.24 = f32[640,1280]{1,0:T(8,128)} copy(f32[640,1280]{1,0:T(8,128)} %get-tuple-element.7) | data formatting | bytes 6553600
Async XLA Ops:
  8.9 5.0 %copy-start = (bf16[640,1280]{1,0:T(8,128)(2,1)S(1)}, bf16[640,1280]{1,0:T(8,128)(2,1)}, u32[]{:S(2)}) copy-start(bf16[640,1280]{1,0:T(8,128)(2,1)} %weight.1) | copy-start | bytes 4915204
  8.9 5.0 %copy-start.1 = (bf16[256,1280]{1,0:T(8,128)(2,1)S(1)}, bf16[256,1280]{1,0:T(8,128)(2,1)}, u32[]{:S(2)}) copy-start(bf16[256,1280]{1,0:T(8,128)(2,1)} %grad_out.1) | copy-start | bytes 1966084
  8.9 5.0 %copy-start.3 = (s32[256,1]{0,1:T(1,128)S(1)}, s32[256,1]{0,1:T(1,128)}, u32[]{:S(2)}) copy-start(s32[256,1]{0,1:T(1,128)} %param.14) | copy-start | bytes 3076
  14.0 1.1 %copy-start.2 = (bf16[256,1280]{1,0:T(8,128)(2,1)S(1)}, bf16[256,1280]{1,0:T(8,128)(2,1)}, u32[]{:S(2)}) copy-start(bf16[256,1280]{1,0:T(8,128)(2,1)} %patches.1) | copy-start | bytes 1966084

commit v3 on v1

v3 whole, which is shorter than its diff:
```python
import functools
import math

import jax
import jax.numpy as jnp
from jax import lax
from jax.experimental import pallas as pl
from jax.experimental.pallas import tpu as pltpu
from jax.sharding import Mesh
from jax.sharding import PartitionSpec as P

HEADS = 16
HEAD_DIM = 80
MESH = pl.DeviceIdType.MESH
ROW, LANE = 16, 128
PARTS = ((4, ("x", "y", "z")), (2, ("y", "x", "z")), (4, ("x", "y", "z")))


def attend_heads(queries, key_in, values, hidden, attended, base):
    width = attended.shape[1]
    pending = {}
    for head in range(width // HEAD_DIM):
        begin = head * HEAD_DIM
        first, last = begin // LANE, (begin + HEAD_DIM - 1) // LANE
        span = (last - first + 1) * LANE
        columns = pl.ds(pl.multiple_of(base + first * LANE, LANE), span)
        place = lax.broadcasted_iota(jnp.int32, (1, span), 1) + (first * LANE - begin)
        own = ((place >= 0) & (place < HEAD_DIM)).astype(jnp.float32).astype(jnp.bfloat16)
        scores = lax.dot_general(
            queries[:, columns] * own, key_in[:, columns], (((1,), (1,)), ((), ())),
            preferred_element_type=jnp.float32,
        ) * (1.0 / math.sqrt(HEAD_DIM)) + hidden[...]
        expo = jnp.exp(scores - jnp.max(scores, axis=1, keepdims=True))
        weights = (expo * (1.0 / jnp.sum(expo, axis=1, keepdims=True))).astype(jnp.bfloat16)
        result = jnp.dot(weights, values[:, columns] * own, preferred_element_type=jnp.float32)
        for block in range(first, last + 1):
            piece = result[:, (block - first) * LANE:(block - first + 1) * LANE]
            pending[block] = pending[block] + piece if block in pending else piece
            if (block + 1) * LANE <= begin + HEAD_DIM:
                attended[:, block * LANE:(block + 1) * LANE] = pending.pop(block).astype(jnp.bfloat16)


class Part:
    def __init__(self, first, blocks, order, sizes, rows):
        self.first, self.blocks, self.order = first, blocks, order
        self.per_block = rows // ROW
        self.tiles = blocks * self.per_block
        n = [sizes[axis] for axis in order]
        self.n = n
        t3 = -(-self.tiles // math.prod(n))
        t2 = -(-self.tiles // (n[0] * n[1]))
        t2 = -(-t2 // t3) * t3
        t1 = n[1] * t2
        self.take = (t1, t2, t3)
        self.owners = (n[0], n[1], t2 // t3)
        self.padded = n[0] * t1
        self.relay = tuple(
            k == 0 and n[k] % 2 == 0 and n[k] >= 4 and self.take[k] >= 2
            for k in range(3)
        )

    def scratch(self):
        held = {"sum0": pltpu.VMEM((self.padded, ROW, LANE), jnp.bfloat16)}
        for k in range(3):
            n, take = self.n[k], self.take[k]
            held[f"in{k}"] = pltpu.VMEM((n - 1, take, ROW, LANE), jnp.bfloat16)
            if k < 2:
                held[f"sum{k + 1}"] = pltpu.VMEM((take, ROW, LANE), jnp.bfloat16)
            for name in ("rs_send", "rs_recv", "ag_send", "ag_recv"):
                held[f"{name}{k}"] = pltpu.SemaphoreType.DMA((n + 2,))
        return held


class Step:
    def __init__(self, part, held, k, bases):
        self.part, self.held, self.k, self.bases = part, held, k, bases
        self.axis, self.n, self.take, self.owners = part.order[k], part.n[k], part.take[k], part.owners[k]
        self.relay, self.everyone = part.relay[k], part.owners[k] == part.n[k]
        self.me = lax.axis_index(self.axis)
        self.far = self.n // 2
        half = self.take // 2
        self.low, self.high = (0, half), (half, self.take - half)
        self.whole = (0, self.take)

    def member(self, d):
        return lax.rem(self.me + d, self.n)

    def run(self, member):
        return (member if self.everyone else jnp.minimum(member, self.owners - 1)) * self.take

    def among(self, member, step):
        if self.everyone:
            step()
        else:
            pl.when(member < self.owners)(step)

    def remote(self, source, target, kind, number, d):
        return pltpu.make_async_remote_copy(
            src_ref=source,
            dst_ref=target,
            send_sem=self.held[f"{kind}_send{self.k}"].at[number],
            recv_sem=self.held[f"{kind}_recv{self.k}"].at[number],
            device_id={self.axis: self.member(d)},
            device_id_type=MESH,
        )

    def given(self):
        if not self.relay:
            return [(d - 1, d, d, self.whole, d - 1) for d in self.nearest_first()], []
        n, far, near = self.n, self.far, self.far - 1
        early = [
            (far - 1, 1, far, self.low, far - 1),
            (n - 1, n - 1, far, self.high, far - 1),
            (near - 1, near, near, self.high, near - 1),
            (n - near - 1, n - near, n - near, self.low, n - near - 1),
        ]
        early += [(d - 1, d, d, self.whole, d - 1) for d in range(1, n) if d not in (near, far, n - near)]
        late = [
            (n, near, near, self.low, near - 1),
            (n + 1, n - near, n - near, self.high, n - near - 1),
        ]
        return early, late

    def nearest_first(self):
        return sorted(range(1, self.n), key=lambda d: -min(d, self.n - d))

    def give(self, copy):
        number, d, owner, (first, count), slot = copy
        start = self.run(self.member(owner)) + first
        return self.remote(
            self.held[f"sum{self.k}"].at[pl.ds(start, count)],
            self.held[f"in{self.k}"].at[slot, pl.ds(first, count)],
            "rs", number, d,
        )

    def reduce_start(self):
        for copy in self.given()[0]:
            self.among(self.member(copy[2]), lambda: self.give(copy).start())

    def reduce_relay(self):
        early, late = self.given()
        for passed, copy in zip(early, late):
            self.give(passed).wait_recv()
            _, _, owner, (first, count), _ = copy
            tiles = pl.ds(self.run(self.member(owner)) + first, count)
            came = self.held[f"in{self.k}"][self.far - 1, pl.ds(first, count)]
            held = self.held[f"sum{self.k}"]
            held[tiles] = (held[tiles].astype(jnp.float32) + came.astype(jnp.float32)).astype(jnp.bfloat16)
            self.give(copy).start()

    def reduce_finish(self):
        k, early, late = self.k, *self.given()

        def receive():
            for copy in early[len(late):] + late:
                self.give(copy).wait_recv()
            total = self.held[f"sum{k}"][pl.ds(self.run(self.me), self.take)].astype(jnp.float32)
            for d in range(1, self.n):
                if not (self.relay and d == self.far):
                    total += self.held[f"in{k}"][d - 1].astype(jnp.float32)
            total = total.astype(jnp.bfloat16)
            if k < 2:
                self.held[f"sum{k + 1}"][...] = total
            else:
                self.held["all"][pl.ds(self.bases[3], self.take)] = total

        self.among(self.me, receive)

    def shown(self):
        if not self.relay:
            return [(d - 1, d, 0, self.whole) for d in self.nearest_first()], []
        n, far, near = self.n, self.far, self.far - 1
        early = [
            (near - 1, near, 0, self.low),
            (n - near - 1, n - near, 0, self.high),
            (n, near, 0, self.high),
            (n + 1, n - near, 0, self.low),
        ]
        early += [(d - 1, d, 0, self.whole) for d in range(1, n) if d not in (near, far, n - near)]
        late = [(far - 1, 1, near, self.low), (n - 1, n - 1, n - near, self.high)]
        return early, late

    def show(self, copy, arriving=False):
        number, d, back, (first, count) = copy
        source = self.member(2 * self.n - back - (d if arriving else 0))
        tiles = pl.ds(self.bases[self.k] + self.run(source) + first, count)
        return self.remote(self.held["all"].at[tiles], self.held["all"].at[tiles], "ag", number, d), source

    def gather_start(self):
        for copy in self.shown()[0]:
            self.among(self.me, lambda: self.show(copy)[0].start())

    def gather_relay(self):
        early, late = self.shown()
        for passed, copy in zip(early, late):
            self.show(passed, True)[0].wait_recv()
            self.show(copy)[0].start()

    def gather_finish(self):
        early, late = self.shown()
        for copy in early[len(late):] + late:
            source = self.member(2 * self.n - copy[2] - copy[1])
            self.among(source, lambda: self.show(copy, True)[0].wait_recv())

    def reduce_drain(self):
        for copy in sum(self.given(), []):
            self.among(self.member(copy[2]), lambda: self.give(copy).wait_send())

    def gather_drain(self):
        for copy in sum(self.shown(), []):
            self.among(self.me, lambda: self.show(copy)[0].wait_send())


def steps_of(parts, scratch):
    steps = [[], [], []]
    for part, held in zip(parts, scratch):
        i1, i2, i3 = (lax.axis_index(axis) for axis in part.order)
        t1, t2, t3 = part.take
        bases = (0, i1 * t1, i1 * t1 + i2 * t2, i1 * t1 + i2 * t2 + i3 * t3)
        for k in range(3):
            steps[k].append(Step(part, held, k, bases))
    return steps


def sum_over_chips(steps, meanwhile):
    for step in steps[0]:
        if step.relay:
            step.reduce_relay()
    write_out = meanwhile()
    for k in range(3):
        for i, step in enumerate(steps[k]):
            step.reduce_finish()
            if k < 2:
                steps[k + 1][i].reduce_start()
            else:
                step.gather_start()
        for step in steps[k]:
            step.reduce_drain()
        if k == 0:
            end = write_out()
    for k in (2, 1, 0):
        for i, step in enumerate(steps[k]):
            if step.relay:
                step.gather_relay()
        for i, step in enumerate(steps[k]):
            step.gather_finish()
            if k > 0:
                steps[k - 1][i].gather_start()
        if k == 1:
            end()
        if k > 0:
            for step in steps[k]:
                step.gather_drain()
    for step in steps[0]:
        step.gather_drain()


def exchange(
    parts, sizes,
    queries, key_in, values, windows_in, owners_in, grad_out, weight, patches,
    returned, *rest,
):
    core = lax.axis_index("fsdp")
    other = 1 - core
    half = weight.shape[0]
    length = queries.shape[0]
    near, scratch = rest[len(parts):]
    scratch = [{**held, "all": total} for held, total in zip(scratch, rest)]
    steps = steps_of(parts, scratch)
    sems = near["sems"]

    barrier = pltpu.get_barrier_semaphore()
    greeted = 0
    for axis, n in sizes.items():
        me = lax.axis_index(axis)
        for d in range(1, n):
            pl.semaphore_signal(
                barrier, inc=1, device_id={axis: lax.rem(me + d, n)}, device_id_type=MESH
            )
            greeted += 1

    def local(source, target, number):
        copy = pltpu.make_async_copy(source, target, sems.at[number])
        copy.start()
        return copy

    windows, owner_ids = near["windows"], near["owners"]
    windows_here = local(windows_in, windows, 12)
    owners_here = local(owners_in, owner_ids, 13)
    grad_out_here = local(grad_out, near["grad_out"].at[0], 0)
    weight_here = local(weight, near["weight"].at[0], 1)
    patches_here = local(patches, near["patches"], 2)

    windows_here.wait()
    ids = jnp.broadcast_to(windows[...].astype(jnp.float32), (length, length))
    near["hidden"][...] = jnp.where(ids == ids.T, 0.0, -1e30)
    arrays = queries, key_in, values, near["hidden"]
    attend_heads(*arrays, near["attended"].at[1], other * half)

    pl.semaphore_wait(barrier, greeted)

    def across(source, target, number):
        copy = pltpu.make_async_remote_copy(
            src_ref=source,
            dst_ref=target,
            send_sem=sems.at[number],
            recv_sem=sems.at[number + 1],
            device_id={"fsdp": other},
            device_id_type=MESH,
        )
        copy.start()
        return copy

    attended_there = across(near["attended"].at[1], near["attended"].at[2], 3)
    grad_out_there = across(grad_out, near["grad_out"].at[1], 5)
    weight_there = across(weight, near["weight"].at[1], 7)
    attend_heads(*arrays, near["attended"].at[0], core * half)

    grad_out_here.wait()
    attended_there.wait_recv()
    grad_out_there.wait_recv()
    rows_in = (((0,), (0,)), ((), ()))
    for part, held, step in zip(parts, scratch, steps[0]):
        columns = pl.ds(part.first * LANE, part.blocks * LANE)
        product = lax.dot_general(
            near["attended"][0], near["grad_out"][0, :, columns], rows_in,
            preferred_element_type=jnp.float32,
        ) + lax.dot_general(
            near["attended"][2], near["grad_out"][1, :, columns], rows_in,
            preferred_element_type=jnp.float32,
        )
        product = product.astype(jnp.bfloat16)
        for block in range(part.blocks):
            held["sum0"][pl.ds(block * part.per_block, part.per_block)] = product[
                :, block * LANE:(block + 1) * LANE
            ].reshape(part.per_block, ROW, LANE)
        spare = part.padded - part.tiles
        if spare:
            held["sum0"][pl.ds(part.tiles, spare)] = jnp.zeros((spare, ROW, LANE), jnp.bfloat16)
        step.reduce_start()

    def encode():
        weight_here.wait()
        patches_here.wait()
        weight_there.wait_recv()
        projected = jnp.dot(
            near["attended"][0], near["weight"][0], preferred_element_type=jnp.float32
        ) + jnp.dot(near["attended"][1], near["weight"][1], preferred_element_type=jnp.float32)
        encoded = (near["patches"][...].astype(jnp.float32) + projected).astype(jnp.bfloat16)
        owners_here.wait()
        owner = owner_ids[...]
        earlier = (
            lax.broadcasted_iota(jnp.int32, (length, length), 0)
            < lax.broadcasted_iota(jnp.int32, (length, length), 1)
        ).astype(jnp.bfloat16)
        is_one = jnp.broadcast_to(owner, (ROW, length)).astype(jnp.float32).astype(jnp.bfloat16)
        ones_before = jnp.dot(is_one, earlier, preferred_element_type=jnp.float32)[:1]
        ones_before = ones_before.astype(jnp.int32)
        place = lax.broadcasted_iota(jnp.int32, (1, length), 1)
        rank = jnp.where(owner == 1, ones_before, place - ones_before)
        slot = lax.broadcasted_iota(jnp.int32, (length, length), 0)

        def placed(group):
            chosen = jnp.where(owner == group, rank, -1)
            onehot = (slot == chosen).astype(jnp.float32).astype(jnp.bfloat16)
            return jnp.dot(onehot, encoded, preferred_element_type=jnp.float32).astype(jnp.bfloat16)

        own_rows = pl.ds(pl.multiple_of(core * length, LANE), length)
        other_rows = pl.ds(pl.multiple_of(other * length, LANE), length)
        near["leaving"][...] = placed(other)
        rows_there = across(near["leaving"], near["returned"].at[own_rows], 9)
        near["returned"][own_rows] = placed(core)

        def write_out():
            rows_there.wait_recv()
            rows_out = local(near["returned"], returned, 11)

            def end():
                rows_there.wait_send()
                rows_out.wait()

            return end

        for copy in (attended_there, grad_out_there, weight_there):
            copy.wait_send()
        return write_out

    sum_over_chips(steps, encode)


def deliver(parts, factor, *refs):
    tiles, (rows, rows_out, gradient, held, sems) = refs[:len(parts)], refs[len(parts):]
    rows_copy = pltpu.make_async_copy(rows, rows_out, sems.at[0])
    rows_copy.start()
    copies = [rows_copy]
    height = held.shape[1]
    deep = height // ROW
    for i in range(held.shape[0]):
        for part, total in zip(parts, tiles):
            for block in range(part.blocks):
                held[i, :, pl.ds((part.first + block) * LANE, LANE)] = (
                    total[pl.ds(block * part.per_block + i * deep, deep)]
                    .reshape(height, LANE).astype(jnp.float32) * factor
                )
        copy = pltpu.make_async_copy(held.at[i], gradient.at[pl.ds(i * height, height)], sems.at[i + 1])
        copy.start()
        copies.append(copy)
    for copy in copies:
        copy.wait()


def per_device(patches, queries, key_in, values, windows, out_weight, owners, grad_out):
    sizes = {axis: lax.axis_size(axis) for axis in ("fsdp", "x", "y", "z")}
    length, width = patches.shape
    half = out_weight.shape[0]
    parts, first = [], 0
    for blocks, order in PARTS:
        parts.append(Part(first, blocks, order, sizes, half))
        first += blocks
    factor = 1.0 / math.sqrt(length * math.prod(sizes.values()))
    bf16 = jnp.bfloat16
    near = {
        "weight": pltpu.VMEM((2, half, width), bf16),
        "patches": pltpu.VMEM((length, width), bf16),
        "windows": pltpu.VMEM((1, length), jnp.int32),
        "owners": pltpu.VMEM((1, length), jnp.int32),
        "hidden": pltpu.VMEM((length, length), jnp.float32),
        "attended": pltpu.VMEM((3, length, half), bf16),
        "grad_out": pltpu.VMEM((2, length, width), bf16),
        "leaving": pltpu.VMEM((length, width), bf16),
        "returned": pltpu.VMEM((2 * length, width), bf16),
        "sems": pltpu.SemaphoreType.DMA((14,)),
    }
    vmem, anywhere, hbm = (
        pl.BlockSpec(memory_space=space) for space in (pltpu.VMEM, pl.ANY, pltpu.HBM)
    )
    params = dict(has_side_effects=True, vmem_limit_bytes=52 * 1024 * 1024)
    returned, *tiles = pl.pallas_call(
        functools.partial(exchange, parts, sizes),
        out_shape=(
            jax.ShapeDtypeStruct((2 * length, width), bf16),
            *(jax.ShapeDtypeStruct((part.padded, ROW, LANE), bf16) for part in parts),
        ),
        in_specs=[vmem] * 3 + [hbm] * 5,
        out_specs=(anywhere, *[vmem] * len(parts)),
        scratch_shapes=[near, [part.scratch() for part in parts]],
        compiler_params=pltpu.CompilerParams(collective_id=0, **params),
        name="exchange",
    )(queries, key_in, values, windows, owners.reshape(1, length), grad_out, out_weight, patches)
    chunks = 4
    return pl.pallas_call(
        functools.partial(deliver, parts, factor),
        out_shape=(
            jax.ShapeDtypeStruct((2 * length, width), bf16),
            jax.ShapeDtypeStruct((half, width), jnp.float32),
        ),
        in_specs=[vmem] * (len(parts) + 1),
        out_specs=(anywhere, anywhere),
        scratch_shapes=[
            pltpu.VMEM((chunks, half // chunks, width), jnp.float32),
            pltpu.SemaphoreType.DMA((chunks + 1,)),
        ],
        compiler_params=pltpu.CompilerParams(**params),
        name="deliver",
    )(*tiles, returned)


def solution(mesh):
    chips = mesh.devices.reshape(12, 8, 4, 2)
    grid = Mesh(chips, ("z", "y", "x", "fsdp"))
    rows = P(("z", "y", "x", "fsdp"), None)
    return jax.shard_map(
        per_device,
        mesh=grid,
        in_specs=(rows, rows, rows, rows, rows, P("fsdp", None), rows, rows),
        out_specs=(rows, P("fsdp", None)),
        check_vma=False,
    )
```

time: 352 us -> 79.4 us (0.23)
  the two profiles are of different devices: /device:TPU:1 before, /device:TPU:2 now
where the time goes in v3:
time: 79.4 us; the launch traced here: 79.2 us
  Pallas kernels  77.2 us (97%)
  local copies, waits for them, and re-layouts  1.35 us (2%)
    pallas_call x1, Pallas kernels, per_device(): pl.pallas_call(functools.partial(exchange, parts, sizes), out_shape=(jax....  73.7 us
    pallas_call x1, Pallas kernels, per_device(): pl.pallas_call(functools.partial(deliver, parts, factor), out_shape=(jax....  3.49 us

profile of v3, /device:TPU:2, one launch (start us, length us, event | category | flops | bytes accessed | tf_op | source)
XLA Modules:
  0.0 79.2 jit_solution(16059582986799249609)
XLA Ops:
  0.6 0.0 copy-start
  0.6 0.7 copy-done
  1.3 0.0 copy-start.1
  1.3 0.7 copy-done.1
  2.0 73.7 %exchange.1 = (bf16[512,1280]{1,0:T(8,128)(2,1)}, bf16[160,16,128]{2,1,0:T(8,128)(2,1)S(1)}, bf16[96,16,128]{2,1,0:T(8,128)(2,1)S(1)}, bf16[160,16,128]{2,1,0:T(8,128)(2,1)S(1)}) custom-call(bf16[256,1280]{1,0:T(8,128)(2,1)} %queries.1, bf16[256,1280]{1,0:T(8,128)(2,1)} %key_in.1, bf16[256,1280]{1,0:T(8,128)(2,1)} %values.1, s32[1,256]{1,0:T(1,128)S(1)} %copy-done, ...), custom_call_target="tpu_custom_call" | custom-call | tf_op jit(solution)/shard_map/exchange/pallas_call | solution.py:438
  75.7 3.5 %deliver.1 = (bf16[512,1280]{1,0:T(8,128)(2,1)}, f32[640,1280]{1,0:T(8,128)}) custom-call(bf16[160,16,128]{2,1,0:T(8,128)(2,1)S(1)} %get-tuple-element.6.refs_0_, bf16[96,16,128]{2,1,0:T(8,128)(2,1)S(1)} %get-tuple-element.7.refs_1_, bf16[160,16,128]{2,1,0:T(8,128)(2,1)S(1)} %get-tuple-element.8.refs_2_, bf16[512,1280]{1,0:T(8,128)(2,1)} %get-tuple-element.9.refs_3_), custom_call_target="tpu_custom_call" | custom-call | tf_op jit(solution)/shard_map/deliver/pallas_call | solution.py:451
Async XLA Ops:
  0.6 0.7 copy-start
  1.3 0.7 copy-start.1

commit v4 on v3

--- a/solution.py
+++ b/solution.py
@@ -257,7 +257,7 @@
 
 def exchange(
     parts, sizes,
-    queries, key_in, values, windows_in, owners_in, grad_out, weight, patches,
+    queries, key_in, values, ids_in, grad_out, weight, patches,
     returned, *rest,
 ):
     core = lax.axis_index("fsdp")
@@ -284,17 +284,20 @@
         copy.start()
         return copy
 
-    windows, owner_ids = near["windows"], near["owners"]
-    windows_here = local(windows_in, windows, 12)
-    owners_here = local(owners_in, owner_ids, 13)
+    ids_here = local(ids_in, near["ids"], 12)
+    arrays_here = [
+        local(array, near["arrays"].at[i], 13 + i) for i, array in enumerate((queries, key_in, values))
+    ]
     grad_out_here = local(grad_out, near["grad_out"].at[0], 0)
     weight_here = local(weight, near["weight"].at[0], 1)
     patches_here = local(patches, near["patches"], 2)
 
-    windows_here.wait()
-    ids = jnp.broadcast_to(windows[...].astype(jnp.float32), (length, length))
+    ids_here.wait()
+    ids = jnp.broadcast_to(near["ids"][0:1].astype(jnp.float32), (length, length))
     near["hidden"][...] = jnp.where(ids == ids.T, 0.0, -1e30)
-    arrays = queries, key_in, values, near["hidden"]
+    for copy in arrays_here:
+        copy.wait()
+    arrays = *(near["arrays"].at[i] for i in range(3)), near["hidden"]
     attend_heads(*arrays, near["attended"].at[1], other * half)
 
     pl.semaphore_wait(barrier, greeted)
@@ -347,8 +350,7 @@
             near["attended"][0], near["weight"][0], preferred_element_type=jnp.float32
         ) + jnp.dot(near["attended"][1], near["weight"][1], preferred_element_type=jnp.float32)
         encoded = (near["patches"][...].astype(jnp.float32) + projected).astype(jnp.bfloat16)
-        owners_here.wait()
-        owner = owner_ids[...]
+        owner = near["ids"][1:2]
         earlier = (
             lax.broadcasted_iota(jnp.int32, (length, length), 0)
             < lax.broadcasted_iota(jnp.int32, (length, length), 1)
@@ -389,10 +391,10 @@
 
 
 def deliver(parts, factor, *refs):
-    tiles, (rows, rows_out, gradient, held, sems) = refs[:len(parts)], refs[len(parts):]
-    rows_copy = pltpu.make_async_copy(rows, rows_out, sems.at[0])
-    rows_copy.start()
-    copies = [rows_copy]
+    tiles, (rows, rows_out, gradient, held, rows_held, sems) = refs[:len(parts)], refs[len(parts):]
+    rows_in = pltpu.make_async_copy(rows, rows_held, sems.at[0])
+    rows_in.start()
+    copies = []
     height = held.shape[1]
     deep = height // ROW
     for i in range(held.shape[0]):
@@ -405,6 +407,11 @@
         copy = pltpu.make_async_copy(held.at[i], gradient.at[pl.ds(i * height, height)], sems.at[i + 1])
         copy.start()
         copies.append(copy)
+        if i == 0:
+            rows_in.wait()
+            rows_copy = pltpu.make_async_copy(rows_held, rows_out, sems.at[held.shape[0] + 1])
+            rows_copy.start()
+            copies.append(rows_copy)
     for copy in copies:
         copy.wait()
 
@@ -422,14 +429,14 @@
     near = {
         "weight": pltpu.VMEM((2, half, width), bf16),
         "patches": pltpu.VMEM((length, width), bf16),
-        "windows": pltpu.VMEM((1, length), jnp.int32),
-        "owners": pltpu.VMEM((1, length), jnp.int32),
+        "ids": pltpu.VMEM((2, length), jnp.int32),
+        "arrays": pltpu.VMEM((3, length, width), bf16),
         "hidden": pltpu.VMEM((length, length), jnp.float32),
         "attended": pltpu.VMEM((3, length, half), bf16),
         "grad_out": pltpu.VMEM((2, length, width), bf16),
         "leaving": pltpu.VMEM((length, width), bf16),
         "returned": pltpu.VMEM((2 * length, width), bf16),
-        "sems": pltpu.SemaphoreType.DMA((14,)),
+        "sems": pltpu.SemaphoreType.DMA((16,)),
     }
     vmem, anywhere, hbm = (
         pl.BlockSpec(memory_space=space) for space in (pltpu.VMEM, pl.ANY, pltpu.HBM)
@@ -441,12 +448,12 @@
             jax.ShapeDtypeStruct((2 * length, width), bf16),
             *(jax.ShapeDtypeStruct((part.padded, ROW, LANE), bf16) for part in parts),
         ),
-        in_specs=[vmem] * 3 + [hbm] * 5,
+        in_specs=[hbm] * 7,
         out_specs=(anywhere, *[vmem] * len(parts)),
         scratch_shapes=[near, [part.scratch() for part in parts]],
         compiler_params=pltpu.CompilerParams(collective_id=0, **params),
         name="exchange",
-    )(queries, key_in, values, windows, owners.reshape(1, length), grad_out, out_weight, patches)
+    )(queries, key_in, values, jnp.stack([windows[0], owners[:, 0]]), grad_out, out_weight, patches)
     chunks = 4
     return pl.pallas_call(
         functools.partial(deliver, parts, factor),
@@ -454,11 +461,12 @@
             jax.ShapeDtypeStruct((2 * length, width), bf16),
             jax.ShapeDtypeStruct((half, width), jnp.float32),
         ),
-        in_specs=[vmem] * (len(parts) + 1),
+        in_specs=[*[vmem] * len(parts), anywhere],
         out_specs=(anywhere, anywhere),
         scratch_shapes=[
             pltpu.VMEM((chunks, half // chunks, width), jnp.float32),
-            pltpu.SemaphoreType.DMA((chunks + 1,)),
+            pltpu.VMEM((2 * length, width), bf16),
+            pltpu.SemaphoreType.DMA((chunks + 2,)),
         ],
         compiler_params=pltpu.CompilerParams(**params),
         name="deliver",

time: 79.4 us -> 77.8 us (0.980)
  the two profiles are of different devices: /device:TPU:2 before, /device:TPU:4 now
where the time goes in v4:
time: 77.8 us; the launch traced here: 77.6 us
  Pallas kernels  76.2 us (98%)
    pallas_call x1, Pallas kernels, per_device(): pl.pallas_call(functools.partial(exchange, parts, sizes), out_shape=(jax....  72.7 us
    pallas_call x1, Pallas kernels, per_device(): pl.pallas_call(functools.partial(deliver, parts, factor), out_shape=(jax....  3.53 us

profile of v4, /device:TPU:4, one launch (start us, length us, event | category | flops | bytes accessed | tf_op | source)
XLA Modules:
  0.0 77.6 jit_solution(17616472834387317848)
XLA Ops:
  0.6 0.7 pad_add_fusion.ids_in
  1.3 72.7 %exchange.1 = (bf16[512,1280]{1,0:T(8,128)(2,1)}, bf16[160,16,128]{2,1,0:T(8,128)(2,1)S(1)}, bf16[96,16,128]{2,1,0:T(8,128)(2,1)S(1)}, bf16[160,16,128]{2,1,0:T(8,128)(2,1)S(1)}) custom-call(bf16[256,1280]{1,0:T(8,128)(2,1)} %queries.1, bf16[256,1280]{1,0:T(8,128)(2,1)} %key_in.1, bf16[256,1280]{1,0:T(8,128)(2,1)} %values.1, ...), custom_call_target="tpu_custom_call" | custom-call | tf_op jit(solution)/shard_map/exchange/pallas_call | solution.py:445
  74.0 3.5 %deliver.1 = (bf16[512,1280]{1,0:T(8,128)(2,1)}, f32[640,1280]{1,0:T(8,128)}) custom-call(bf16[160,16,128]{2,1,0:T(8,128)(2,1)S(1)} %get-tuple-element.6.refs_0_, bf16[96,16,128]{2,1,0:T(8,128)(2,1)S(1)} %get-tuple-element.7.refs_1_, bf16[160,16,128]{2,1,0:T(8,128)(2,1)S(1)} %get-tuple-element.8.refs_2_, bf16[512,1280]{1,0:T(8,128)(2,1)} %get-tuple-element.9.refs_3_), custom_call_target="tpu_custom_call" | custom-call | tf_op jit(solution)/shard_map/deliver/pallas_call | solution.py:458

commit v5 on v4

--- a/solution.py
+++ b/solution.py
@@ -299,6 +299,7 @@
         copy.wait()
     arrays = *(near["arrays"].at[i] for i in range(3)), near["hidden"]
     attend_heads(*arrays, near["attended"].at[1], other * half)
+    near["turned"][1] = near["attended"][1].T
 
     pl.semaphore_wait(barrier, greeted)
 
@@ -314,23 +315,21 @@
         copy.start()
         return copy
 
-    attended_there = across(near["attended"].at[1], near["attended"].at[2], 3)
+    attended_there = across(near["turned"].at[1], near["turned"].at[2], 3)
     grad_out_there = across(grad_out, near["grad_out"].at[1], 5)
     weight_there = across(weight, near["weight"].at[1], 7)
     attend_heads(*arrays, near["attended"].at[0], core * half)
+    near["turned"][0] = near["attended"][0].T
 
     grad_out_here.wait()
     attended_there.wait_recv()
     grad_out_there.wait_recv()
-    rows_in = (((0,), (0,)), ((), ()))
     for part, held, step in zip(parts, scratch, steps[0]):
         columns = pl.ds(part.first * LANE, part.blocks * LANE)
-        product = lax.dot_general(
-            near["attended"][0], near["grad_out"][0, :, columns], rows_in,
-            preferred_element_type=jnp.float32,
-        ) + lax.dot_general(
-            near["attended"][2], near["grad_out"][1, :, columns], rows_in,
-            preferred_element_type=jnp.float32,
+        product = jnp.dot(
+            near["turned"][0], near["grad_out"][0, :, columns], preferred_element_type=jnp.float32
+        ) + jnp.dot(
+            near["turned"][2], near["grad_out"][1, :, columns], preferred_element_type=jnp.float32
         )
         product = product.astype(jnp.bfloat16)
         for block in range(part.blocks):
@@ -391,9 +390,7 @@
 
 
 def deliver(parts, factor, *refs):
-    tiles, (rows, rows_out, gradient, held, rows_held, sems) = refs[:len(parts)], refs[len(parts):]
-    rows_in = pltpu.make_async_copy(rows, rows_held, sems.at[0])
-    rows_in.start()
+    tiles, (gradient, held, sems) = refs[:len(parts)], refs[len(parts):]
     copies = []
     height = held.shape[1]
     deep = height // ROW
@@ -404,14 +401,9 @@
                     total[pl.ds(block * part.per_block + i * deep, deep)]
                     .reshape(height, LANE).astype(jnp.float32) * factor
                 )
-        copy = pltpu.make_async_copy(held.at[i], gradient.at[pl.ds(i * height, height)], sems.at[i + 1])
+        copy = pltpu.make_async_copy(held.at[i], gradient.at[pl.ds(i * height, height)], sems.at[i])
         copy.start()
         copies.append(copy)
-        if i == 0:
-            rows_in.wait()
-            rows_copy = pltpu.make_async_copy(rows_held, rows_out, sems.at[held.shape[0] + 1])
-            rows_copy.start()
-            copies.append(rows_copy)
     for copy in copies:
         copy.wait()
 
@@ -432,7 +424,8 @@
         "ids": pltpu.VMEM((2, length), jnp.int32),
         "arrays": pltpu.VMEM((3, length, width), bf16),
         "hidden": pltpu.VMEM((length, length), jnp.float32),
-        "attended": pltpu.VMEM((3, length, half), bf16),
+        "attended": pltpu.VMEM((2, length, half), bf16),
+        "turned": pltpu.VMEM((3, half, length), bf16),
         "grad_out": pltpu.VMEM((2, length, width), bf16),
         "leaving": pltpu.VMEM((length, width), bf16),
         "returned": pltpu.VMEM((2 * length, width), bf16),
@@ -455,22 +448,19 @@
         name="exchange",
     )(queries, key_in, values, jnp.stack([windows[0], owners[:, 0]]), grad_out, out_weight, patches)
     chunks = 4
-    return pl.pallas_call(
+    gradient = pl.pallas_call(
         functools.partial(deliver, parts, factor),
-        out_shape=(
-            jax.ShapeDtypeStruct((2 * length, width), bf16),
-            jax.ShapeDtypeStruct((half, width), jnp.float32),
-        ),
-        in_specs=[*[vmem] * len(parts), anywhere],
-        out_specs=(anywhere, anywhere),
+        out_shape=jax.ShapeDtypeStruct((half, width), jnp.float32),
+        in_specs=[vmem] * len(parts),
+        out_specs=anywhere,
         scratch_shapes=[
             pltpu.VMEM((chunks, half // chunks, width), jnp.float32),
-            pltpu.VMEM((2 * length, width), bf16),
-            pltpu.SemaphoreType.DMA((chunks + 2,)),
+            pltpu.SemaphoreType.DMA((chunks,)),
         ],
         compiler_params=pltpu.CompilerParams(**params),
         name="deliver",
-    )(*tiles, returned)
+    )(*tiles)
+    return returned, gradient
 
 
 def solution(mesh):

time: 77.8 us -> 77.4 us (level)
  Pallas kernels: 76.2 us -> 74.6 us
  local copies, waits for them, and re-layouts: 0 us -> 1.32 us
    pallas_call x1, Pallas kernels: 3.53 us -> 1.8 us  [per_device(): pl.pallas_call(functools.partial(deliver, parts, factor), out_shape=jax.S...]
    unnamed x0 -> x3, local copies, waits for them, and re-layouts: none -> 1.32 us
where the time goes in v5:
time: 77.4 us; the launch traced here: 77.2 us
  Pallas kernels  74.6 us (96%)
  local copies, waits for them, and re-layouts  1.32 us (2%)
    pallas_call x1, Pallas kernels, per_device(): pl.pallas_call(functools.partial(exchange, parts, sizes), out_shape=(jax....  72.8 us
    pallas_call x1, Pallas kernels, per_device(): pl.pallas_call(functools.partial(deliver, parts, factor), out_shape=jax.S...  1.8 us

profile of v5, /device:TPU:4, one launch (start us, length us, event | category | flops | bytes accessed | tf_op | source)
XLA Modules:
  0.0 77.2 jit_solution(3595075575870414138)
XLA Ops:
  0.6 0.7 pad_add_fusion.ids_in
  1.3 72.8 %exchange.1 = (bf16[512,1280]{1,0:T(8,128)(2,1)}, bf16[160,16,128]{2,1,0:T(8,128)(2,1)S(1)}, bf16[96,16,128]{2,1,0:T(8,128)(2,1)S(1)}, bf16[160,16,128]{2,1,0:T(8,128)(2,1)S(1)}) custom-call(bf16[256,1280]{1,0:T(8,128)(2,1)} %queries.1, bf16[256,1280]{1,0:T(8,128)(2,1)} %key_in.1, bf16[256,1280]{1,0:T(8,128)(2,1)} %values.1, ...), custom_call_target="tpu_custom_call" | custom-call | tf_op jit(solution)/shard_map/exchange/pallas_call | solution.py:438
  74.1 0.0 copy-start
  74.1 1.8 %deliver.1 = f32[640,1280]{1,0:T(8,128)} custom-call(bf16[160,16,128]{2,1,0:T(8,128)(2,1)S(1)} %get-tuple-element.7.refs_0_, bf16[96,16,128]{2,1,0:T(8,128)(2,1)S(1)} %get-tuple-element.8.refs_1_, bf16[160,16,128]{2,1,0:T(8,128)(2,1)S(1)} %get-tuple-element.9.refs_2_), custom_call_target="tpu_custom_call" | custom-call | tf_op jit(solution)/shard_map/deliver/pallas_call | solution.py:451
  75.9 0.3 copy-done
  76.2 1.1 %copy.11 = bf16[512,1280]{1,0:T(8,128)(2,1)} copy(bf16[512,1280]{1,0:T(8,128)(2,1)S(1)} %copy-done) | data formatting | bytes 2621440
Async XLA Ops:
  74.1 2.1 %copy-start = (bf16[512,1280]{1,0:T(8,128)(2,1)S(1)}, bf16[512,1280]{1,0:T(8,128)(2,1)}, u32[]{:S(2)}) copy-start(bf16[512,1280]{1,0:T(8,128)(2,1)} %get-tuple-element.12) | copy-start | bytes 3932164
